TPU v7x, 32 devices: a whole 2x2x4 slice. The times are simulated.
32 devices in a mesh: shell: 4 (over x, core), tile: 8 (over z, y).
Axes of the slice: x: 2, y: 2, z: 4, core: 2. Of those that a mesh axis runs over, the one named last changes fastest.
Arguments:
- sky_grad: float32 [10, 8192, 128], P(None, ('tile', 'shell')), may hold values from -6 to 6
- kernel: float32 [10, 8], replicated, may hold values from 0.05 to 1
- owner_dev: int32 [8, 8192, 1], P('shell', 'tile'), may hold values from 0 to 7; in each aligned block of 1024 rows (0 to 1023, 1024 to 2047, ..., all dimensions but the last counted through in order) at most 512 rows name the same one
- cell_index: int32 [8, 8192], P('shell', 'tile'), may hold values from 0 to 255
- level_index: int32 [8, 8192], P('shell', 'tile'), may hold values from 0 to 255
Outputs:
- shell_grad: float32 [8, 2048, 128], P('shell', 'tile')
Inputs may be any that keep to these rules, and one draw needn't show every extreme that they name: `owner_dev`: among the 1024 sky blocks of one sky tile and one shell, no owner is named more than 512 times, a bound that some block reaches.
All inputs are finite; a program needn't handle non-finite values.
Results may differ from a plain program's by a relative error of at most 0.00007.
Values sent between devices are 32-bit elements; how exact they have to be, the bound alone decides.
A program may use at most 64 MiB of HBM per device.

v0:
```python
import jax
import jax.numpy as jnp
from jax import lax
from jax.sharding import PartitionSpec as P

LEVELS = 256
BLK_DEV = 256
RB = 16


def shards(sky_grad, kernel, owner_dev, cell_index, level_index):
    shells_here = owner_dev.shape[0]
    group_id = lax.axis_index("shell")
    whole_sky = lax.all_gather(sky_grad, "shell", axis=1, tiled=True)
    my_kernel = lax.dynamic_slice_in_dim(kernel, group_id * shells_here, shells_here, 1)
    reduced = jnp.einsum("bs,brc->src", my_kernel, whole_sky, precision=lax.Precision.HIGHEST)
    owner_ids = owner_dev[:, :, 0]
    fraction = (level_index.astype(jnp.float32) + 0.5) / LEVELS
    destination = owner_ids * BLK_DEV + cell_index
    targets = lax.broadcasted_iota(jnp.int32, (1, lax.axis_size("tile") * BLK_DEV, 1), 1)
    weights = jnp.where(destination[:, None, :] == targets, (1.0 - fraction)[:, None, :], 0.0)
    weights = weights + jnp.where(
        destination[:, None, :] + RB == targets, fraction[:, None, :], 0.0
    )
    summed = lax.psum_scatter(
        jnp.einsum("str,src->tsc", weights, reduced, precision=lax.Precision.HIGHEST),
        "tile",
        scatter_dimension=0,
        tiled=True,
    )
    return jnp.transpose(summed, (1, 0, 2))


def solution(mesh):
    return jax.shard_map(
        shards,
        mesh=mesh,
        in_specs=(
            P(None, ("tile", "shell"), None),
            P(),
            P("shell", "tile", None),
            P("shell", "tile"),
            P("shell", "tile"),
        ),
        out_specs=P("shell", "tile", None),
        check_vma=False,
    )
```

profile of v0, /device:TPU:12, one launch (start us, length us, event | category | flops | bytes accessed | tf_op | source)
XLA Modules:
  0.0 159.8 jit_solution(3918855680210807439)
XLA Ops:
  6.5 0.0 copy-start
  6.5 0.0 all-gather.2.cloned.1.call-start
  6.5 0.7 all-gather.2.cloned.1.call-update
  7.3 0.0 reduce-scatter.2.cloned.1.call-start
  7.3 0.7 broadcast_subtract_fusion
  8.0 0.7 broadcast_add_fusion
  8.7 41.8 %all-gather.2.cloned.1.call-done = f32[10,1024,128]{2,1,0:T(8,128)} async-done(((f32[10,256,128]{2,1,0:T(8,128)}), f32[10,1024,128]{2,1,0:T(8,128)}) %all-gather.2.cloned.1.call-update) | async-done | bytes 5242896 | tf_op jit(solution)/shard_map/all_gather | solution.py:14
  50.5 0.0 copy-done
  50.5 10.3 %fusion.4 = f32[2,1024,128]{2,0,1:T(2,128)S(1)} fusion(f32[10,1024,128]{2,1,0:T(8,128)} %all-gather.2.cloned.1.call-done, f32[10,8]{0,1:T(8,128)S(1)} %copy-done, s32[]{:T(128)S(6)} %select_n.10), kind=kOutput, calls=%fused_computation.6 | convolution fusion | flops 31457280 | bytes 6292484 | tf_op jit(solution)/shard_map/bs,brc->src/dot_general | solution.py:16
  60.8 22.7 %fusion.11 = f32[2048,2,128]{0,2,1:T(8,128)} fusion(f32[2,1024]{1,0:T(2,128)S(1)} %get-tuple-element.8, s32[2,1024]{1,0:T(2,128)S(1)} %get-tuple-element.5, f32[2,1024]{1,0:T(2,128)S(1)} %get-tuple-element.7, s32[2,1024]{1,0:T(2,128)S(1)} %get-tuple-element.6, f32[2,1024,128]{2,0,1:T(2,128)S(1)} %fusion.4), kind=kOutput, calls=%fused_computation.13 | convolution fusion | flops 6463422464 | bytes 3178496 | tf_op jit(solution)/shard_map/str,src->tsc/dot_general | solution.py:26
  83.5 0.0 reduce-scatter.2.cloned.1.call-update
  83.5 67.7 %reduce-scatter.2.cloned.1.call-done = f32[256,2,128]{0,2,1:T(8,128)} async-done(((f32[2048,2,128]{0,2,1:T(8,128)}), f32[256,2,128]{0,2,1:T(8,128)}) %reduce-scatter.2.cloned.1.call-update) | async-done | bytes 262160 | tf_op jit(solution)/shard_map/reduce_scatter | solution.py:25
  151.2 1.8 %copy.7 = f32[2,256,128]{2,1,0:T(8,128)} copy(f32[2,256,128]{1,2,0:T(8,128)} %bitcast.9) | data formatting | bytes 524288 | tf_op jit(solution)/shard_map/transpose | solution.py:31
Async XLA Ops:
  6.5 44.0 %copy-start = (f32[10,8]{0,1:T(8,128)S(1)}, f32[10,8]{0,1:T(8,128)}, u32[]{:S(2)}) copy-start(f32[10,8]{0,1:T(8,128)} %param.6) | copy-start | bytes 964
  6.5 44.0 %all-gather.2.cloned.1.call-start = ((), (), s32[]{:S(2)}) async-start(), calls=%async_computation.1 | async-start | bytes 6553600 | tf_op jit(solution)/shard_map/all_gather | solution.py:14
  7.3 143.9 %reduce-scatter.2.cloned.1.call-start = ((), (), s32[]{:S(2)}) async-start(), calls=%async_computation.2 | async-start | bytes 2359296 | tf_op jit(solution)/shard_map/reduce_scatter | solution.py:25
Sparse Core Ops, SparseCore 0:
  8.9 41.5 all-gather.1
  83.6 67.5 reduce-scatter.1
where the time goes:
time: 162 us; the launch traced here: 160 us
  waiting for transfers between devices  110 us (68%)
  matrix products  33 us (20%)
  between operations  13.4 us (8%)
  local copies, waits for them, and re-layouts  1.79 us (1%)
    reduce_scatter x1, waiting for transfers between devices, shards(): lax.psum_scatter(jnp.einsum('str,src->tsc', weights, reduced, precision=l...  67.7 us
    all_gather x1, waiting for transfers between devices, shards(): whole_sky = lax.all_gather(sky_grad, 'shell', axis=1, tiled=True)  41.8 us
    dot_general x1, matrix products, shards(): jnp.einsum('str,src->tsc', weights, reduced, precision=lax.Precision.HIGH...  22.7 us
    dot_general x1, matrix products, shards(): jnp.einsum('bs,brc->src', my_kernel, whole_sky, precision=lax.Precision.H...  10.3 us
  transfers between devices with their start and end apart: 2, of which 2 were waited for; matrix products, arithmetic and copies ran while one was open for 1% of the time, Pallas kernels for 0%

commit v1 on v0

v1 whole, which is shorter than its diff:
```python
import functools
import math

import jax
import jax.numpy as jnp
from jax import lax
from jax.experimental import pallas as pl
from jax.experimental.pallas import tpu as pltpu
from jax.sharding import PartitionSpec as P

LEVELS = 256
BLK_DEV = 256
RB = 16
EXT = BLK_DEV + RB
LANES = 128
MESH = pl.DeviceIdType.MESH


def body(
    groups, near, far,
    sky_hbm, kern, index, out,
    sky, red, rows, halves, index_all, part, landed,
    load_sem, send_sem, recv_sem, index_send, index_recv, far_send, far_recv,
):
    bins, here, _ = sky.shape
    per_group = rows.shape[0]
    group = lax.axis_index("shell")
    tile = lax.axis_index("tile")
    hi = tile // near
    lo = tile % near

    def device(group_to, hi_to, lo_to):
        return {"shell": group_to, "tile": hi_to * near + lo_to}

    load = pltpu.make_async_copy(sky_hbm, sky, load_sem)
    load.start()

    barrier = pltpu.get_barrier_semaphore()
    peers = [(d, e) for d in range(groups) for e in range(near) if (d, e) != (0, 0)]
    for d, e in peers:
        pl.semaphore_signal(
            barrier, inc=1, device_id_type=MESH,
            device_id=device((group + d) % groups, hi, (lo + e) % near),
        )
    for f in range(1, far):
        pl.semaphore_signal(
            barrier, inc=1, device_id_type=MESH, device_id=device(group, (hi + f) % far, lo)
        )

    def row_copy(s, d, e):
        return pltpu.make_async_remote_copy(
            src_ref=red.at[s, d],
            dst_ref=rows.at[s, lo, pl.ds(pl.multiple_of(group * here, here), here)],
            send_sem=send_sem.at[s, d, e],
            recv_sem=recv_sem.at[s, d, e],
            device_id=device((group + d) % groups, hi, (lo + e) % near),
            device_id_type=MESH,
        )

    def index_copy(e):
        return pltpu.make_async_remote_copy(
            src_ref=index,
            dst_ref=index_all.at[lo],
            send_sem=index_send.at[e],
            recv_sem=index_recv.at[e],
            device_id=device(group, hi, (lo + e) % near),
            device_id_type=MESH,
        )

    def far_copy(s, to, slot):
        return pltpu.make_async_remote_copy(
            src_ref=part.at[s, to],
            dst_ref=landed.at[s, slot],
            send_sem=far_send.at[s, to],
            recv_sem=far_recv.at[s, slot],
            device_id=device(group, to, lo),
            device_id_type=MESH,
        )

    def reduce_bins(s, d):
        shell = ((group + d) % groups) * per_group + s
        total = kern[0, shell] * sky[0]
        for b in range(1, bins):
            total = total + kern[b, shell] * sky[b]
        return total

    index_all[lo] = index[...]
    load.wait()
    order = sorted(range(groups), key=lambda d: (d == 0, abs(d - groups // 2)))
    for s in range(per_group):
        for n, d in enumerate(order):
            red[s, d] = reduce_bins(s, d)
            if s == 0 and n == 0:
                pl.semaphore_wait(barrier, len(peers) + far - 1)
                for e in range(1, near):
                    index_copy(e).start()
            for e in reversed(range(near)):
                if (d, e) != (0, 0):
                    row_copy(s, d, e).start()
        rows[s, lo, pl.ds(pl.multiple_of(group * here, here), here)] = red[s, 0]

    for e in range(1, near):
        index_copy(e).wait()

    low_half = hi < far // 2
    flipped = jnp.where(low_half, hi, far - 1 - hi)
    above = far - 1 - flipped
    for s in range(per_group):
        for d, e in peers:
            row_copy(s, d, e).wait_recv()
        for n in range(near):
            whole = rows[s, n]
            top = whole.astype(jnp.bfloat16)
            halves[n, :, :LANES] = top
            halves[n, :, LANES:] = (whole - top.astype(jnp.float32)).astype(jnp.bfloat16)

        @pl.loop(0, far)
        def _(k):
            to = jnp.where(k < above, far - 1 - k, k - above)
            to = jnp.where(low_half, to, far - 1 - to)
            first = (to * near + lo) * BLK_DEV - RB
            total = jnp.zeros((2 * EXT, 2 * LANES), jnp.float32)
            for n in range(near):
                place = index_all[n, s : s + 1, :] - first
                level = index_all[n, per_group + s : per_group + s + 1, :].astype(jnp.float32)
                level = jnp.broadcast_to(level * (1.0 / LEVELS), (EXT, level.shape[1]))
                hit = lax.broadcasted_iota(jnp.int32, (EXT, place.shape[1]), 0) == place
                ones = jnp.where(hit, 1.0, 0.0).astype(jnp.bfloat16)
                levels = jnp.where(hit, level, 0.0).astype(jnp.bfloat16)
                total = total + jnp.dot(
                    jnp.concatenate([ones, levels], axis=0), halves[n],
                    preferred_element_type=jnp.float32,
                )
            total = total[:, :LANES] + total[:, LANES:]
            landing = total[:EXT]
            shifted = total[EXT:] + landing * (0.5 / LEVELS)
            part[s, to] = landing[RB:] - shifted[RB:] + shifted[:BLK_DEV]

            @pl.when(to != hi)
            def _():
                far_copy(s, to, hi).start()

    for s in range(per_group):
        total = part[s, hi]
        for f in range(1, far):
            source = (hi + f) % far
            far_copy(s, source, source).wait_recv()
            total = total + landed[s, source]
        out[s] = total

    for s in range(per_group):
        for d, e in peers:
            row_copy(s, d, e).wait_send()
        for f in range(1, far):
            to = (hi + f) % far
            far_copy(s, to, to).wait_send()


def shards(near, sky_grad, kernel, owner_dev, cell_index, level_index):
    groups, tiles = lax.axis_size("shell"), lax.axis_size("tile")
    far = tiles // near
    bins, here, lanes = sky_grad.shape
    per_group, tile_rows = cell_index.shape
    index = jnp.concatenate([owner_dev[:, :, 0] * BLK_DEV + cell_index, level_index], axis=0)
    f32 = jnp.float32
    vmem = pl.BlockSpec(memory_space=pltpu.VMEM)
    return pl.pallas_call(
        functools.partial(body, groups, near, far),
        out_shape=jax.ShapeDtypeStruct((per_group, BLK_DEV, lanes), f32),
        in_specs=[
            pl.BlockSpec(memory_space=pl.ANY),
            pl.BlockSpec(memory_space=pltpu.SMEM),
            vmem,
        ],
        out_specs=vmem,
        scratch_shapes=[
            pltpu.VMEM((bins, here, lanes), f32),
            pltpu.VMEM((per_group, groups, here, lanes), f32),
            pltpu.VMEM((per_group, near, tile_rows, lanes), f32),
            pltpu.VMEM((near, tile_rows, 2 * lanes), jnp.bfloat16),
            pltpu.VMEM((near, 2 * per_group, tile_rows), jnp.int32),
            pltpu.VMEM((per_group, far, BLK_DEV, lanes), f32),
            pltpu.VMEM((per_group, far, BLK_DEV, lanes), f32),
            pltpu.SemaphoreType.DMA,
            pltpu.SemaphoreType.DMA((per_group, groups, near)),
            pltpu.SemaphoreType.DMA((per_group, groups, near)),
            pltpu.SemaphoreType.DMA((near,)),
            pltpu.SemaphoreType.DMA((near,)),
            pltpu.SemaphoreType.DMA((per_group, far)),
            pltpu.SemaphoreType.DMA((per_group, far)),
        ],
        compiler_params=pltpu.CompilerParams(
            collective_id=0, has_side_effects=True, vmem_limit_bytes=40 << 20
        ),
    )(sky_grad, kernel, index)


def solution(mesh):
    near = 1 << (int(math.log2(mesh.shape["tile"])) // 2)
    return jax.shard_map(
        functools.partial(shards, near),
        mesh=mesh,
        in_specs=(
            P(None, ("tile", "shell"), None),
            P(),
            P("shell", "tile", None),
            P("shell", "tile"),
            P("shell", "tile"),
        ),
        out_specs=P("shell", "tile", None),
        check_vma=False,
    )
```

time: 162 us -> 49.8 us (0.31); the launches traced: 160 us -> 49.4 us
  waiting for transfers between devices: 110 us -> 0 us
  Pallas kernels: 0 us -> 45.2 us
  matrix products: 33 us -> 0 us
  between operations: 13.4 us -> 0.02 us
    reduce_scatter x1 -> x0, waiting for transfers between devices: 67.7 us -> none  [shards(): lax.psum_scatter(jnp.einsum('str,src->tsc', weights, reduced, precision=l...]
    pallas_call x0 -> x1, Pallas kernels: none -> 45.2 us  [shards(): pl.pallas_call(functools.partial(body, groups, near, far), out_shape=jax....]
    all_gather x1 -> x0, waiting for transfers between devices: 41.8 us -> none  [shards(): whole_sky = lax.all_gather(sky_grad, 'shell', axis=1, tiled=True)]
    dot_general x2 -> x0, matrix products: 33 us -> none  [the longest x1 22.7 us: shards(): jnp.einsum('str,src->tsc', weights, reduced, precision=lax.Precision.HIGH...]
    unnamed x2 -> x4, local copies, waits for them, and re-layouts: 0.01 us -> 2.79 us
    transpose x1 -> x0, local copies, waits for them, and re-layouts: 1.78 us -> none  [shards(): return jnp.transpose(summed, (1, 0, 2))]
  transfers between devices with their start and end apart: 2 -> 0, of which waited for: 2 -> 0; matrix products, arithmetic and copies ran while one was open for 1% -> 0% of each run, Pallas kernels for 0% -> 0%
where the time goes in v1:
time: 49.8 us; the launch traced here: 49.4 us
  Pallas kernels  45.2 us (91%)
  local copies, waits for them, and re-layouts  2.79 us (6%)
  other arithmetic  1.43 us (3%)
    pallas_call x1, Pallas kernels, shards(): pl.pallas_call(functools.partial(body, groups, near, far), out_shape=jax....  45.2 us
    unnamed x4, local copies, waits for them, and re-layouts  2.79 us

profile of v1, /device:TPU:12, one launch (start us, length us, event | category | flops | bytes accessed | tf_op | source)
XLA Modules:
  0.0 49.4 jit_solution(9387711992693906760)
XLA Ops:
  0.0 0.8 %copy.7.kern = f32[10,8]{1,0:T(8,128)S(1)} copy(f32[10,8]{0,1:T(8,128)} %param.6) | data formatting | bytes 640 | tf_op args[1]
  0.8 0.7 %bitcast_add_fusion = s32[2,1024]{1,0:T(2,128)S(1)} fusion(s32[2,1024]{1,0:T(2,128)} %param.8, s32[2,1024,1]{1,2,0:T(1,128)} %param.7), kind=kLoop, calls=%fused_computation.1 | loop fusion | flops 4096 | bytes 24576 | tf_op jit(solution)/shard_map/add | solution.py:164
  1.5 0.7 %pad_add_fusion.index = s32[4,1024]{1,0:T(4,128)S(1)} fusion(s32[2,1024]{1,0:T(2,128)} %param.9, s32[2,1024]{1,0:T(2,128)S(1)} %bitcast_add_fusion), kind=kLoop, calls=%fused_computation | loop fusion | flops 4096 | bytes 32768 | tf_op jit(solution)/shard_map/concatenate | solution.py:164
  2.2 0.0 copy-start
  2.2 1.3 %copy-done = f32[10,256,128]{2,1,0:T(8,128)S(1)} copy-done((f32[10,256,128]{2,1,0:T(8,128)S(1)}, f32[10,256,128]{2,1,0:T(8,128)}, u32[]{:S(2)}) %copy-start) | copy-done | bytes 1310744
  3.5 45.2 %shard_map.55 = f32[2,256,128]{2,1,0:T(8,128)S(1)} custom-call(f32[10,256,128]{2,1,0:T(8,128)S(1)} %copy-done, f32[10,8]{1,0:T(8,128)S(1)} %copy.7.kern, s32[4,1024]{1,0:T(4,128)S(1)} %pad_add_fusion.index), custom_call_target="tpu_custom_call" | custom-call | tf_op jit(solution)/shard_map/pallas_call | solution.py:167
  48.7 0.7 %copy.12 = f32[2,256,128]{2,1,0:T(8,128)} copy(f32[2,256,128]{2,1,0:T(8,128)S(1)} %shard_map.55) | data formatting | bytes 524288
Async XLA Ops:
  2.2 1.3 %copy-start = (f32[10,256,128]{2,1,0:T(8,128)S(1)}, f32[10,256,128]{2,1,0:T(8,128)}, u32[]{:S(2)}) copy-start(f32[10,256,128]{2,1,0:T(8,128)} %sky_hbm.1) | copy-start | bytes 3932164

commit v2 on v1

--- a/solution.py
+++ b/solution.py
@@ -18,9 +18,9 @@
 
 def body(
     groups, near, far,
-    sky_hbm, kern, index, out,
-    sky, red, rows, halves, index_all, part, landed,
-    load_sem, send_sem, recv_sem, index_send, index_recv, far_send, far_recv,
+    sky_hbm, kern, owner_hbm, cell_hbm, level_hbm, out,
+    sky, owner, cell, level_in, index, red, rows, halves, index_all, part, landed, relay,
+    load_sem, send_sem, recv_sem, index_send, index_recv, far_send, far_recv, relay_recv,
 ):
     bins, here, _ = sky.shape
     per_group = rows.shape[0]
@@ -29,11 +29,36 @@
     hi = tile // near
     lo = tile % near
 
+    low_half = hi < far // 2
+    flipped = jnp.where(low_half, hi, far - 1 - hi)
+    relayed = far >= 4
+    visits = []
+    for h in range(max(1, far // 2)):
+        others = sorted((t for t in range(far) if t != h), key=lambda t: (-abs(t - h), t))
+        if relayed and h == 1:
+            others = [t for t in others if t != far - 1] + [h, far - 1]
+        else:
+            others = others + [h]
+        visits.append(others)
+
+    def visit(k):
+        to = jnp.int32(0)
+        for h, others in enumerate(visits):
+            for n, t in enumerate(others):
+                to = jnp.where((flipped == h) & (k == n), t, to)
+        return jnp.where(low_half, to, far - 1 - to)
+
     def device(group_to, hi_to, lo_to):
         return {"shell": group_to, "tile": hi_to * near + lo_to}
 
-    load = pltpu.make_async_copy(sky_hbm, sky, load_sem)
-    load.start()
+    loads = [
+        pltpu.make_async_copy(source, target, load_sem.at[n])
+        for n, (source, target) in enumerate(
+            [(sky_hbm, sky), (owner_hbm, owner), (cell_hbm, cell), (level_hbm, level_in)]
+        )
+    ]
+    for load in loads:
+        load.start()
 
     barrier = pltpu.get_barrier_semaphore()
     peers = [(d, e) for d in range(groups) for e in range(near) if (d, e) != (0, 0)]
@@ -77,15 +102,30 @@
             device_id_type=MESH,
         )
 
+    def relay_copy(s, to):
+        return pltpu.make_async_remote_copy(
+            src_ref=part.at[s, to],
+            dst_ref=relay.at[s],
+            send_sem=far_send.at[s, to],
+            recv_sem=relay_recv.at[s],
+            device_id=device(group, jnp.where(low_half, 1, far - 2), lo),
+            device_id_type=MESH,
+        )
+
     def reduce_bins(s, d):
         shell = ((group + d) % groups) * per_group + s
-        total = kern[0, shell] * sky[0]
+        total = kern[shell, 0] * sky[0]
         for b in range(1, bins):
-            total = total + kern[b, shell] * sky[b]
+            total = total + kern[shell, b] * sky[b]
         return total
 
+    for load in loads[1:]:
+        load.wait()
+    for s in range(per_group):
+        index[s : s + 1, :] = owner[s] * BLK_DEV + cell[s : s + 1, :]
+        index[per_group + s : per_group + s + 1, :] = level_in[s : s + 1, :]
     index_all[lo] = index[...]
-    load.wait()
+    loads[0].wait()
     order = sorted(range(groups), key=lambda d: (d == 0, abs(d - groups // 2)))
     for s in range(per_group):
         for n, d in enumerate(order):
@@ -102,9 +142,6 @@
     for e in range(1, near):
         index_copy(e).wait()
 
-    low_half = hi < far // 2
-    flipped = jnp.where(low_half, hi, far - 1 - hi)
-    above = far - 1 - flipped
     for s in range(per_group):
         for d, e in peers:
             row_copy(s, d, e).wait_recv()
@@ -116,8 +153,7 @@
 
         @pl.loop(0, far)
         def _(k):
-            to = jnp.where(k < above, far - 1 - k, k - above)
-            to = jnp.where(low_half, to, far - 1 - to)
+            to = visit(k)
             first = (to * near + lo) * BLK_DEV - RB
             total = jnp.zeros((2 * EXT, 2 * LANES), jnp.float32)
             for n in range(near):
@@ -136,17 +172,30 @@
             shifted = total[EXT:] + landing * (0.5 / LEVELS)
             part[s, to] = landing[RB:] - shifted[RB:] + shifted[:BLK_DEV]
 
-            @pl.when(to != hi)
+            ends = (to == jnp.where(low_half, far - 1, 0)) & relayed
+
+            @pl.when(ends & (flipped == 1))
+            def _():
+                relay_copy(s, to).wait_recv()
+                part[s, to] += relay[s]
+
+            @pl.when(ends & (flipped == 0))
+            def _():
+                relay_copy(s, to).start()
+
+            @pl.when((to != hi) & jnp.logical_not(ends & (flipped == 0)))
             def _():
                 far_copy(s, to, hi).start()
 
     for s in range(per_group):
-        total = part[s, hi]
+        out[s] = part[s, hi]
         for f in range(1, far):
             source = (hi + f) % far
-            far_copy(s, source, source).wait_recv()
-            total = total + landed[s, source]
-        out[s] = total
+
+            @pl.when(jnp.logical_not(relayed & (jnp.abs(source - hi) == far - 1)))
+            def _():
+                far_copy(s, source, source).wait_recv()
+                out[s] += landed[s, source]
 
     for s in range(per_group):
         for d, e in peers:
@@ -161,38 +210,39 @@
     far = tiles // near
     bins, here, lanes = sky_grad.shape
     per_group, tile_rows = cell_index.shape
-    index = jnp.concatenate([owner_dev[:, :, 0] * BLK_DEV + cell_index, level_index], axis=0)
     f32 = jnp.float32
-    vmem = pl.BlockSpec(memory_space=pltpu.VMEM)
+    hbm = pl.BlockSpec(memory_space=pl.ANY)
     return pl.pallas_call(
         functools.partial(body, groups, near, far),
         out_shape=jax.ShapeDtypeStruct((per_group, BLK_DEV, lanes), f32),
-        in_specs=[
-            pl.BlockSpec(memory_space=pl.ANY),
-            pl.BlockSpec(memory_space=pltpu.SMEM),
-            vmem,
-        ],
-        out_specs=vmem,
+        in_specs=[hbm, pl.BlockSpec(memory_space=pltpu.SMEM), hbm, hbm, hbm],
+        out_specs=pl.BlockSpec(memory_space=pltpu.VMEM),
         scratch_shapes=[
             pltpu.VMEM((bins, here, lanes), f32),
+            pltpu.VMEM((per_group, 1, tile_rows), jnp.int32),
+            pltpu.VMEM((per_group, tile_rows), jnp.int32),
+            pltpu.VMEM((per_group, tile_rows), jnp.int32),
+            pltpu.VMEM((2 * per_group, tile_rows), jnp.int32),
             pltpu.VMEM((per_group, groups, here, lanes), f32),
             pltpu.VMEM((per_group, near, tile_rows, lanes), f32),
             pltpu.VMEM((near, tile_rows, 2 * lanes), jnp.bfloat16),
             pltpu.VMEM((near, 2 * per_group, tile_rows), jnp.int32),
             pltpu.VMEM((per_group, far, BLK_DEV, lanes), f32),
             pltpu.VMEM((per_group, far, BLK_DEV, lanes), f32),
-            pltpu.SemaphoreType.DMA,
+            pltpu.VMEM((per_group, BLK_DEV, lanes), f32),
+            pltpu.SemaphoreType.DMA((4,)),
             pltpu.SemaphoreType.DMA((per_group, groups, near)),
             pltpu.SemaphoreType.DMA((per_group, groups, near)),
             pltpu.SemaphoreType.DMA((near,)),
             pltpu.SemaphoreType.DMA((near,)),
             pltpu.SemaphoreType.DMA((per_group, far)),
             pltpu.SemaphoreType.DMA((per_group, far)),
+            pltpu.SemaphoreType.DMA((per_group,)),
         ],
         compiler_params=pltpu.CompilerParams(
-            collective_id=0, has_side_effects=True, vmem_limit_bytes=40 << 20
+            collective_id=0, has_side_effects=True, vmem_limit_bytes=56 << 20
         ),
-    )(sky_grad, kernel, index)
+    )(sky_grad, kernel.T, owner_dev.transpose(0, 2, 1), cell_index, level_index)
 
 
 def solution(mesh):

time: 49.8 us -> 46 us (0.924)
  the two profiles are of different devices: /device:TPU:12 before, /device:TPU:0 now
where the time goes in v2:
time: 46 us; the launch traced here: 45.8 us
  Pallas kernels  44.1 us (96%)
  local copies, waits for them, and re-layouts  1.67 us (4%)
    pallas_call x1, Pallas kernels, shards(): pl.pallas_call(functools.partial(body, groups, near, far), out_shape=jax....  44.1 us
    unnamed x1, local copies, waits for them, and re-layouts  1.67 us

profile of v2, /device:TPU:0, one launch (start us, length us, event | category | flops | bytes accessed | tf_op | source)
XLA Modules:
  0.0 45.8 jit_solution(12478662599654730700)
XLA Ops:
  0.0 44.1 %shard_map.55 = f32[2,256,128]{2,1,0:T(8,128)} custom-call(f32[10,256,128]{2,1,0:T(8,128)} %sky_hbm.1, f32[8,10]{1,0:T(8,128)} %bitcast.3, s32[2,1,1024]{2,1,0:T(1,128)} %bitcast.2, s32[2,1024]{1,0:T(2,128)} %cell_hbm.1, s32[2,1024]{1,0:T(2,128)} %level_hbm.1), custom_call_target="tpu_custom_call" | custom-call | tf_op jit(solution)/shard_map/pallas_call | solution.py:215
  44.1 1.7 %copy.7 = f32[2,256,128]{2,1,0:T(8,128)} copy(f32[2,256,128]{2,1,0:T(8,128)} %shard_map.55) | data formatting | bytes 524288

commit v3 on v2

v3 whole, which is shorter than its diff:
```python
import functools
import math

import jax
import jax.numpy as jnp
from jax import lax
from jax.experimental import pallas as pl
from jax.experimental.pallas import tpu as pltpu
from jax.sharding import PartitionSpec as P

LEVELS = 256
BLK_DEV = 256
RB = 16
EXT = BLK_DEV + RB
LANES = 128
MESH = pl.DeviceIdType.MESH


def body(
    groups, near, far,
    sky_hbm, kern, owner_hbm, cell_hbm, level_hbm, out,
    sky, owner, cell, level_in, index, red, rows, halves, part, landed, near_part, near_landed,
    load_sem, send_sem, recv_sem, far_send, far_recv, near_send, near_recv,
):
    bins, here, _ = sky.shape
    per_group = rows.shape[0]
    group = lax.axis_index("shell")
    tile = lax.axis_index("tile")
    hi = tile // near
    lo = tile % near

    low_half = hi < far // 2
    flipped = jnp.where(low_half, hi, far - 1 - hi)
    visits = []
    for h in range(max(1, far // 2)):
        visits.append(sorted((t for t in range(far) if t != h), key=lambda t: (-abs(t - h), t)) + [h])

    def visit(k):
        to = jnp.int32(0)
        for h, others in enumerate(visits):
            for n, t in enumerate(others):
                to = jnp.where((flipped == h) & (k == n), t, to)
        return jnp.where(low_half, to, far - 1 - to)

    def device(group_to, hi_to, lo_to):
        return {"shell": group_to, "tile": hi_to * near + lo_to}

    loads = [
        pltpu.make_async_copy(source, target, load_sem.at[n])
        for n, (source, target) in enumerate(
            [(sky_hbm, sky), (owner_hbm, owner), (cell_hbm, cell), (level_hbm, level_in)]
        )
    ]
    for load in loads:
        load.start()

    barrier = pltpu.get_barrier_semaphore()
    peers = [(d, e) for d in range(groups) for e in range(near) if (d, e) != (0, 0)]
    peers_of = [[(d, 0) for d in range(1, groups)]] * per_group
    for d, e in peers:
        pl.semaphore_signal(
            barrier, inc=1, device_id_type=MESH,
            device_id=device((group + d) % groups, hi, (lo + e) % near),
        )
    for f in range(1, far):
        pl.semaphore_signal(
            barrier, inc=1, device_id_type=MESH, device_id=device(group, (hi + f) % far, lo)
        )

    def row_copy(s, d, e):
        return pltpu.make_async_remote_copy(
            src_ref=red.at[s, d],
            dst_ref=rows.at[s, lo, pl.ds(pl.multiple_of(group * here, here), here)],
            send_sem=send_sem.at[s, d, e],
            recv_sem=recv_sem.at[s, d, e],
            device_id=device((group + d) % groups, hi, (lo + e) % near),
            device_id_type=MESH,
        )

    def near_copy(s, e, to):
        return pltpu.make_async_remote_copy(
            src_ref=near_part.at[s, e, to],
            dst_ref=near_landed.at[s, e, to],
            send_sem=near_send.at[s, e, to],
            recv_sem=near_recv.at[s, e, to],
            device_id=device(group, hi, (lo + e) % near),
            device_id_type=MESH,
        )

    def far_copy(s, to, slot):
        return pltpu.make_async_remote_copy(
            src_ref=part.at[s, to],
            dst_ref=landed.at[s, slot],
            send_sem=far_send.at[s, to],
            recv_sem=far_recv.at[s, slot],
            device_id=device(group, to, lo),
            device_id_type=MESH,
        )

    def reduce_bins(s, d):
        shell = ((group + d) % groups) * per_group + s
        total = kern[shell, 0] * sky[0]
        for b in range(1, bins):
            total = total + kern[shell, b] * sky[b]
        return total

    for load in loads[1:]:
        load.wait()
    for s in range(per_group):
        index[s : s + 1, :] = owner[s] * BLK_DEV + cell[s : s + 1, :]
        index[per_group + s : per_group + s + 1, :] = level_in[s : s + 1, :]
    loads[0].wait()
    order = sorted(range(groups), key=lambda d: (d == 0, abs(d - groups // 2)))
    for s in range(per_group):
        for n, d in enumerate(order):
            red[s, d] = reduce_bins(s, d)
            if s == 0 and n == 0:
                pl.semaphore_wait(barrier, len(peers) + far - 1)
            for e in reversed(range(near)):
                if (d, e) in peers_of[s]:
                    row_copy(s, d, e).start()
        rows[s, lo, pl.ds(pl.multiple_of(group * here, here), here)] = red[s, 0]

    def split(s, slot, n):
        whole = rows[s, n]
        top = whole.astype(jnp.bfloat16)
        halves[slot, :, :LANES] = top
        halves[slot, :, LANES:] = (whole - top.astype(jnp.float32)).astype(jnp.bfloat16)

    def deposit(s, indices, to, lo_to):
        first = (to * near + lo_to) * BLK_DEV - RB
        total = jnp.zeros((2 * EXT, 2 * LANES), jnp.float32)
        for slot, there in enumerate(indices):
            place = there[s : s + 1, :] - first
            level = there[per_group + s : per_group + s + 1, :].astype(jnp.float32)
            level = jnp.broadcast_to(level * (1.0 / LEVELS), (EXT, level.shape[1]))
            hit = lax.broadcasted_iota(jnp.int32, (EXT, place.shape[1]), 0) == place
            ones = jnp.where(hit, 1.0, 0.0).astype(jnp.bfloat16)
            levels = jnp.where(hit, level, 0.0).astype(jnp.bfloat16)
            total = total + jnp.dot(
                jnp.concatenate([ones, levels], axis=0), halves[slot],
                preferred_element_type=jnp.float32,
            )
        total = total[:, :LANES] + total[:, LANES:]
        landing = total[:EXT]
        shifted = total[EXT:] + landing * (0.5 / LEVELS)
        return landing[RB:] - shifted[RB:] + shifted[:BLK_DEV]

    def send_far(s, to):
        @pl.when(to != hi)
        def _():
            far_copy(s, to, hi).start()

    def near_sum(s, k):
        to = visit(k)
        for e in range(1, near):
            near_copy(s, e, to).wait_recv()
            part[s, to] += near_landed[s, e, to]
        send_far(s, to)

    def near_part_send(s):
        for d, e in peers_of[s]:
            row_copy(s, d, e).wait_recv()
        split(s, 0, lo)

        @pl.loop(0, far)
        def _(k):
            to = visit(k)
            for e in range(1, near):
                near_part[s, e, to] = deposit(s, [index], to, (lo + e) % near)
                near_copy(s, e, to).start()

    def own_part(s):
        @pl.loop(0, far)
        def _(k):
            to = visit(k)
            part[s, to] = deposit(s, [index], to, lo)

    for s in range(per_group):
        near_part_send(s)
        own_part(s)
        if s > 0:
            pl.loop(far // 2, far)(functools.partial(near_sum, s - 1))
        if s < per_group - 1:
            pl.loop(0, far // 2)(functools.partial(near_sum, s))
    pl.loop(0, far)(functools.partial(near_sum, per_group - 1))

    for s in range(per_group):
        out[s] = part[s, hi]
        for f in range(1, far):
            source = (hi + f) % far
            far_copy(s, source, source).wait_recv()
            out[s] += landed[s, source]

    for s in range(per_group):
        for d, e in peers_of[s]:
            row_copy(s, d, e).wait_send()
        for f in range(1, far):
            to = (hi + f) % far
            far_copy(s, to, to).wait_send()
    for e in range(1, near):
        for to in range(far):
            for s in range(per_group):
                near_copy(s, e, to).wait_send()


def shards(near, sky_grad, kernel, owner_dev, cell_index, level_index):
    groups, tiles = lax.axis_size("shell"), lax.axis_size("tile")
    far = tiles // near
    bins, here, lanes = sky_grad.shape
    per_group, tile_rows = cell_index.shape
    f32 = jnp.float32
    hbm = pl.BlockSpec(memory_space=pl.ANY)
    return pl.pallas_call(
        functools.partial(body, groups, near, far),
        out_shape=jax.ShapeDtypeStruct((per_group, BLK_DEV, lanes), f32),
        in_specs=[hbm, pl.BlockSpec(memory_space=pltpu.SMEM), hbm, hbm, hbm],
        out_specs=pl.BlockSpec(memory_space=pltpu.VMEM),
        scratch_shapes=[
            pltpu.VMEM((bins, here, lanes), f32),
            pltpu.VMEM((per_group, 1, tile_rows), jnp.int32),
            pltpu.VMEM((per_group, tile_rows), jnp.int32),
            pltpu.VMEM((per_group, tile_rows), jnp.int32),
            pltpu.VMEM((2 * per_group, tile_rows), jnp.int32),
            pltpu.VMEM((per_group, groups, here, lanes), f32),
            pltpu.VMEM((per_group, near, tile_rows, lanes), f32),
            pltpu.VMEM((near, tile_rows, 2 * lanes), jnp.bfloat16),
            pltpu.VMEM((per_group, far, BLK_DEV, lanes), f32),
            pltpu.VMEM((per_group, far, BLK_DEV, lanes), f32),
            pltpu.VMEM((per_group, near, far, BLK_DEV, lanes), f32),
            pltpu.VMEM((per_group, near, far, BLK_DEV, lanes), f32),
            pltpu.SemaphoreType.DMA((4,)),
            pltpu.SemaphoreType.DMA((per_group, groups, near)),
            pltpu.SemaphoreType.DMA((per_group, groups, near)),
            pltpu.SemaphoreType.DMA((per_group, far)),
            pltpu.SemaphoreType.DMA((per_group, far)),
            pltpu.SemaphoreType.DMA((per_group, near, far)),
            pltpu.SemaphoreType.DMA((per_group, near, far)),
        ],
        compiler_params=pltpu.CompilerParams(
            collective_id=0, has_side_effects=True, vmem_limit_bytes=56 << 20
        ),
    )(sky_grad, kernel.T, owner_dev.transpose(0, 2, 1), cell_index, level_index)


def solution(mesh):
    near = 1 << (int(math.log2(mesh.shape["tile"])) // 2)
    return jax.shard_map(
        functools.partial(shards, near),
        mesh=mesh,
        in_specs=(
            P(None, ("tile", "shell"), None),
            P(),
            P("shell", "tile", None),
            P("shell", "tile"),
            P("shell", "tile"),
        ),
        out_specs=P("shell", "tile", None),
        check_vma=False,
    )
```

time: 46 us -> 44.2 us (0.961)
  the two profiles are of different devices: /device:TPU:0 before, /device:TPU:12 now
where the time goes in v3:
time: 44.2 us; the launch traced here: 43.8 us
  Pallas kernels  42.1 us (95%)
  local copies, waits for them, and re-layouts  1.67 us (4%)
    pallas_call x1, Pallas kernels, shards(): pl.pallas_call(functools.partial(body, groups, near, far), out_shape=jax....  42.1 us
    unnamed x1, local copies, waits for them, and re-layouts  1.67 us

profile of v3, /device:TPU:12, one launch (start us, length us, event | category | flops | bytes accessed | tf_op | source)
XLA Modules:
  0.0 43.8 jit_solution(4671478035089751728)
XLA Ops:
  0.0 42.1 %shard_map.55 = f32[2,256,128]{2,1,0:T(8,128)} custom-call(f32[10,256,128]{2,1,0:T(8,128)} %sky_hbm.1, f32[8,10]{1,0:T(8,128)} %bitcast.3, s32[2,1,1024]{2,1,0:T(1,128)} %bitcast.2, s32[2,1024]{1,0:T(2,128)} %cell_hbm.1, s32[2,1024]{1,0:T(2,128)} %level_hbm.1), custom_call_target="tpu_custom_call" | custom-call | tf_op jit(solution)/shard_map/pallas_call | solution.py:214
  42.1 1.7 %copy.7 = f32[2,256,128]{2,1,0:T(8,128)} copy(f32[2,256,128]{2,1,0:T(8,128)} %shard_map.55) | data formatting | bytes 524288
